TPU v7x, 128 devices: a whole 4x4x4 slice. The times are simulated.
128 devices in a mesh: tile: 8 (over y_hi, z), phase: 16 (over x, y_lo, core).
Axes of the slice: x: 4, y: 4 (y_hi: 2, y_lo: 2; y = y_hi * 2 + y_lo), z: 4, core: 2. Of those that a mesh axis runs over, the one named last changes fastest.
Arguments:
- latent: bfloat16 [1, 256, 256, 640], P(None, 'tile', 'phase'), may hold values from -6 to 6
- previous: bfloat16 [1, 128, 128, 640], P(None, 'tile', 'phase'), may hold values from -6 to 6
- blend_weight: float32 [256, 256], P('tile', 'phase'), may hold values from 0.2 to 0.8
- skip_weight: float32 [256, 256], P('tile', 'phase'), may hold values from 0.1 to 0.5
- norm_gain: float32 [640], replicated, may hold values from 0.5 to 7, as said below
- w_query: bfloat16 [640, 640], replicated, may hold values from -0.25 to 0.25
- w_key: bfloat16 [640, 640], replicated, may hold values from -0.25 to 0.25
- w_value: bfloat16 [640, 640], replicated, may hold values from -0.25 to 0.25
- w_out: bfloat16 [640, 640], replicated, may hold values from -3.59375 to 3.59375
Outputs:
- result: bfloat16 [1, 256, 256, 640], P(None, 'tile', 'phase')
Inputs may be any that keep to these rules, and one draw needn't show every extreme that they name: `norm_gain`: positive gains, one a channel.
All inputs are finite; a program needn't handle non-finite values.
Results may differ from a plain program's by a relative error of at most 0.007.
The roundings to bfloat16 on the way count: a program that leaves them out, or rounds other values in their place, can miss the bound.
Values may be sent and summed in bfloat16 or wider, within the bound.
A program may use at most 128 MiB of HBM per device.

v0:
```python
import jax
import jax.numpy as jnp
from jax import lax
from jax.sharding import PartitionSpec as P

HEADS = 10
STRIDE = 4
OV = 16


def padded(block, sides, width):
    for axis, dim in sides:
        count = lax.axis_size(axis)
        forward = [(i, i + 1) for i in range(count - 1)]
        backward = [(target, source) for source, target in forward]
        low = lax.ppermute(
            lax.slice_in_dim(block, block.shape[dim] - width, None, axis=dim), axis, forward
        )
        high = lax.ppermute(lax.slice_in_dim(block, 0, width, axis=dim), axis, backward)
        block = jnp.concatenate([low, block, high], axis=dim)
    return block


def layer_norm(tensor, gain_vector):
    widened = tensor.astype(jnp.float32)
    average = jnp.mean(widened, axis=-1, keepdims=True)
    centred = widened - average
    variance = jnp.mean(centred * centred, axis=-1, keepdims=True)
    return (centred * lax.rsqrt(variance + 1e-05) * gain_vector).astype(jnp.bfloat16)


def project(tensor, matrix):
    return jnp.dot(tensor, matrix, preferred_element_type=jnp.float32).astype(jnp.bfloat16)


def attend(queries, key_rows, value_rows, inside):
    head_size = queries.shape[1] // HEADS
    factor = head_size ** (-0.5)

    def one_head(head_index):
        first_col = head_index * head_size
        query_head = lax.dynamic_slice_in_dim(queries, first_col, head_size, 1)
        key_head = lax.dynamic_slice_in_dim(key_rows, first_col, head_size, 1)
        value_head = lax.dynamic_slice_in_dim(value_rows, first_col, head_size, 1)
        scores = jnp.dot(query_head, key_head.T, preferred_element_type=jnp.float32) * factor
        scores = jnp.where(inside[None, :], scores, -1e30)
        largest = jnp.max(scores, axis=1, keepdims=True)
        raised = jnp.exp(scores - largest)
        weights = (raised / jnp.sum(raised, axis=1, keepdims=True)).astype(jnp.bfloat16)
        return jnp.dot(weights, value_head, preferred_element_type=jnp.float32)

    stacked = lax.map(one_head, jnp.arange(HEADS, dtype=jnp.int32))
    return stacked.transpose(1, 0, 2).reshape(queries.shape[0], -1)


def to_phases(tensor):
    image_count, row_count, col_count, channels = tensor.shape
    split = tensor.reshape(
        image_count, row_count // STRIDE, STRIDE, col_count // STRIDE, STRIDE, channels
    )
    return split.transpose(2, 4, 0, 1, 3, 5).reshape(
        STRIDE * STRIDE, image_count, row_count // STRIDE, col_count // STRIDE, channels
    )


def from_phases(tensor, target):
    split = tensor.reshape((STRIDE, STRIDE) + tensor.shape[1:])
    return split.transpose(2, 3, 0, 4, 1, 5).reshape(target)


def shards(latent, previous, blend_weight, skip_weight, norm_gain, w_query, w_key, w_value, w_out):
    image_count, row_count, col_count, channels = latent.shape
    normed = layer_norm(latent, norm_gain)
    w_pair = jnp.concatenate([w_key, w_value], axis=1)
    queries = project(normed, w_query)
    paired = project(normed, w_pair)
    widened = padded(paired, (("tile", 1), ("phase", 2)), OV)
    row_where = (
        lax.axis_index("tile") * row_count - OV + jnp.arange(row_count + 2 * OV, dtype=jnp.int32)
    )
    col_where = (
        lax.axis_index("phase") * col_count - OV + jnp.arange(col_count + 2 * OV, dtype=jnp.int32)
    )
    row_inside = (row_where >= 0) & (row_where < row_count * lax.axis_size("tile"))
    col_inside = (col_where >= 0) & (col_where < col_count * lax.axis_size("phase"))
    inside = (row_inside[:, None] & col_inside[None, :]).reshape(-1)

    def per_image(couple):
        flat_pair = couple[1].reshape(-1, 2 * channels)
        return attend(
            couple[0].reshape(-1, channels),
            flat_pair[:, :channels],
            flat_pair[:, channels:],
            inside,
        )

    local_out = lax.map(per_image, (queries, widened)).reshape(latent.shape)
    sub_normed = lax.all_to_all(to_phases(normed), "phase", split_axis=0, concat_axis=3, tiled=True)
    sub_query = project(sub_normed, w_query)
    all_pairs = project(lax.all_gather(sub_normed, "tile", axis=2, tiled=True), w_pair)
    held_count = sub_query.shape[0]
    flat_query = sub_query.reshape(held_count * image_count, -1, channels)
    flat_pairs = all_pairs.reshape(held_count * image_count, -1, 2 * channels)
    inside_all = jnp.ones((flat_pairs.shape[1],), dtype=bool)

    def per_phase(couple):
        return attend(
            couple[0], couple[1][:, :channels], couple[1][:, channels:], inside_all
        ).astype(jnp.bfloat16)

    dilated = lax.map(per_phase, (flat_query, flat_pairs)).reshape(sub_query.shape)
    returned = lax.all_to_all(dilated, "phase", split_axis=3, concat_axis=0, tiled=True)
    dilated_here = from_phases(returned, latent.shape)
    mixing = blend_weight[None, :, :, None]
    mixed_rows = ((1.0 - mixing) * local_out + mixing * dilated_here.astype(jnp.float32)).astype(
        jnp.bfloat16
    )
    attention = jnp.dot(mixed_rows, w_out, preferred_element_type=jnp.float32)
    upsampled = jnp.repeat(jnp.repeat(previous, 2, axis=1), 2, axis=2).astype(jnp.float32)
    keeping = skip_weight[None, :, :, None]
    return (
        (1.0 - keeping) * (latent.astype(jnp.float32) + attention) + keeping * upsampled
    ).astype(jnp.bfloat16)


def solution(mesh):
    return jax.shard_map(
        shards,
        mesh=mesh,
        in_specs=(
            P(None, "tile", "phase", None),
            P(None, "tile", "phase", None),
            P("tile", "phase"),
            P("tile", "phase"),
            P(),
            P(),
            P(),
            P(),
            P(),
        ),
        out_specs=P(None, "tile", "phase", None),
        check_vma=False,
    )
```

profile of v0, /device:TPU:1, one launch (start us, length us, event | category | flops | bytes accessed | tf_op | source)
XLA Modules:
  0.0 399.8 jit_solution(6441854944364756465)
XLA Ops:
  11.1 18.4 %all_to_all.30 = bf16[16,1,8,4,640]{4,3,2,1,0:T(4,128)(2,1)S(1)} all-to-all(bf16[16,1,8,4,640]{4,3,2,1,0:T(4,128)(2,1)S(1)} %bitcast.93), channel_id=1, replica_groups=mesh['tile'=8,'phase'=16] {'phase'}, dimensions={0} | all-to-all | bytes 1310720 | tf_op jit(solution)/shard_map/all_to_all | solution.py:98
  34.1 3.6 collective-permute-start
  39.0 17.7 %collective-permute-done = bf16[1,16,16,1280]{3,2,1,0:T(8,128)(2,1)S(1)} collective-permute-done((bf16[1,16,16,1280]{3,2,1,0:T(8,128)(2,1)S(1)}, bf16[1,16,16,1280]{3,2,1,0:T(8,128)(2,1)S(1)}, u32[]{:S(2)}, u32[]{:S(2)}) %collective-permute-start) | collective-permute-done | bytes 655392 | tf_op jit(solution)/shard_map/ppermute | solution.py:16
  56.7 8.8 %collective-permute-done.1 = bf16[1,16,16,1280]{3,2,1,0:T(8,128)(2,1)S(1)} collective-permute-done((bf16[1,16,16,1280]{3,2,1,0:T(8,128)(2,1)S(1)}, bf16[1,16,16,1280]{3,2,1,0:T(8,128)(2,1)S(1)}, u32[]{:S(2)}, u32[]{:S(2)}) %collective-permute-start.1) | collective-permute-done | bytes 655392 | tf_op jit(solution)/shard_map/ppermute | solution.py:19
  67.3 4.0 %collective-permute-start.2 = (bf16[1,64,16,1280]{3,2,1,0:T(8,128)(2,1)}, bf16[1,64,16,1280]{3,2,1,0:T(8,128)(2,1)}, u32[]{:S(2)}, u32[]{:S(2)}) collective-permute-start(bf16[1,64,16,1280]{3,2,1,0:T(8,128)(2,1)} %pad_maximum_fusion.1), channel_id=1, source_target_pairs={{0,1},{1,2},{2,3},{3,4},{4,5},{5,6},{6,7},{7,8},{8,9},{9,10},{10,1... | collective-permute-start | bytes 7864328 | tf_op jit(solution)/shard_map/ppermute | solution.py:16
  84.8 71.6 %collective-permute-done.2 = bf16[1,64,16,1280]{3,2,1,0:T(8,128)(2,1)} collective-permute-done((bf16[1,64,16,1280]{3,2,1,0:T(8,128)(2,1)}, bf16[1,64,16,1280]{3,2,1,0:T(8,128)(2,1)}, u32[]{:S(2)}, u32[]{:S(2)}) %collective-permute-start.2) | collective-permute-done | bytes 2621472 | tf_op jit(solution)/shard_map/ppermute | solution.py:16
  156.4 7.3 %pad_maximum_fusion = bf16[1,64,48,1280]{3,2,1,0:T(8,128)(2,1)S(1)} fusion(bf16[1,64,16,1280]{3,2,1,0:T(8,128)(2,1)} %collective-permute-done.3, bf16[1,16,16,1280]{3,2,1,0:T(8,128)(2,1)S(1)} %copy-done.8, bf16[1,32,16,1280]{3,2,1,0:T(8,128)(2,1)S(1)} %fusion.27, bf16[1,16,16,1280]{3,2,1,0:T(8,128)(2,1)S(1)} %copy-done.6, ...), kind=kLoop, calls=%fused_computation.33 | loop fusion | flops 39321600 | bytes 15728640 | tf_op jit(solution)/shard_map/concatenate | solution.py:20
  163.7 3.7 fusion.47
  167.4 14.6 %convolution_convert_fusion = bf16[64,64,1280]{2,1,0:T(8,128)(2,1)} fusion(bf16[1,1,64,64,640]{4,3,1,0,2:T(8,128)(2,1)} %all-gather.2.cloned.1.call-done, bf16[640,640]{1,0:T(8,128)(2,1)S(1)} %copy-done.16, bf16[640,640]{1,0:T(8,128)(2,1)S(1)} %copy-done.17), kind=kOutput, calls=%fused_computation.32 | convolution fusion | flops 6719406080 | bytes 17367040 | tf_op jit(solution)/shard_map/dot_general | solution.py:33
  182.1 8.8 %fusion.46 = (bf16[4096,640]{1,0:T(8,128)(2,1)}, bf16[4096,640]{1,0:T(8,128)(2,1)}) fusion(bf16[4096,1280]{1,0:T(8,128)(2,1)} %bitcast.89), kind=kLoop, calls=%fused_computation.72 | loop fusion | bytes 20971520 | tf_op jit(solution)/shard_map/while/body/eval_jaxpr/slice | solution.py:108
  190.9 89.9 %while.37 = (s32[]{:T(128)}, bf16[10,512,64]{1,2,0:T(8,128)(2,1)S(1)}, s32[10]{0:T(128)S(1)}, bf16[512,640]{1,0:T(8,128)(2,1)}, bf16[4096,640]{1,0:T(8,128)(2,1)}, /*index=5*/bf16[4096,640]{1,0:T(8,128)(2,1)}, s32[1]{0:T(128)}) while((s32[]{:T(128)}, bf16[10,512,64]{1,2,0:T(8,128)(2,1)S(1)}, s32[10]{0:T(128)S(1)}, ...), condition=%wide.region_9.10_spmd.clone, body=%wide.region_6.9_spmd.sunk.clone | while | flops 555744256 | bytes 27537036 | solution.py:52
  196.3 3.5 fusion.65
  205.3 3.5 fusion.65
  223.3 3.5 fusion.65
  232.3 3.5 fusion.65
  250.3 3.5 fusion.65
  259.2 3.5 fusion.65
  283.4 4.7 %all-to-all-start.1 = ((bf16[1,1,8,64,640]{4,2,1,0,3:T(8,128)(2,1)}), bf16[1,1,8,64,640]{4,2,1,0,3:T(8,128)(2,1)S(1)}, u32[]{:S(2)}, u32[]{:S(2)}) async-start(bf16[1,1,8,64,640]{4,2,1,0,3:T(8,128)(2,1)} %copy.42), calls=%async_computation.1 | async-start | bytes 1310720 | tf_op jit(solution)/shard_map/all_to_all | solution.py:112
  288.1 89.4 %while.38 = (s32[]{:T(128)}, f32[10,512,64]{1,2,0:T(8,128)}, s32[10]{0:T(128)S(1)}, bf16[512,640]{1,0:T(8,128)(2,1)}, bf16[3072,640]{1,0:T(8,128)(2,1)}, /*index...) while((s32[]{:T(128)}, f32[10,512,64]{1,2,0:T(8,128)}, ...), condition=%wide.region_5.6_spmd.clone.clone, body=%wide.region_2.5_spmd.clone.sunk.clone | while | flops 421529600 | bytes 20739852 | solution.py:52
  293.3 3.7 fusion.69
  302.3 3.7 fusion.69
  311.2 3.7 fusion.69
  320.2 3.7 fusion.69
  329.1 3.7 fusion.69
  338.0 3.7 fusion.69
  347.0 3.7 fusion.69
  355.9 3.7 fusion.69
  364.9 3.7 fusion.69
  373.8 3.7 fusion.69
  377.5 4.7 %copy.36 = f32[512,10,64]{2,1,0:T(8,128)} copy(f32[512,10,64]{0,2,1:T(8,128)} %bitcast.98) | data formatting | bytes 2621440 | tf_op jit(solution)/shard_map/while/body/eval_jaxpr/transpose | solution.py:53
  382.2 4.1 %reshape.178 = f32[32,16,640]{2,1,0:T(8,128)} reshape(f32[512,10,64]{2,1,0:T(8,128)} %copy.36) | data formatting | bytes 2621440 | tf_op jit(solution)/shard_map/reshape | solution.py:97
  389.0 4.0 %fusion.32 = bf16[1,32,16,640]{3,2,1,0:T(8,128)(2,1)} fusion(bf16[1,32,16,640]{3,2,1,0:T(8,128)(2,1)S(1)} %copy-done.2, f32[1,32,16,640]{3,2,1,0:T(8,128)} %convert_element_type.116, bf16[640,640]{1,0:T(8,128)(2,1)} %param.21, f32[32,16,640]{2,1,0:T(8,128)} %reshape.183, f32[32,16,640]{2,1,0:T(8,128)} %reshape.178, f32[32,16]{1,0:T(8,128)S(1)} %copy-done.10, ...), kind=kOutput, calls=%fused_computation.47 | convolution fusion | flops 422707200 | bytes 6070272 | tf_op jit(solution)/shard_map/dot_general | solution.py:118
  (162 shorter events, 138.8 us)
Async XLA Ops:
  6.5 72.9 %copy-start = (bf16[640,640]{1,0:T(8,128)(2,1)S(1)}, bf16[640,640]{1,0:T(8,128)(2,1)}, u32[]{:S(2)}) copy-start(bf16[640,640]{1,0:T(8,128)(2,1)} %param.18) | copy-start | bytes 2457604
  6.5 160.9 %all-gather.2.cloned.1.call-start = ((), (), s32[]{:S(2)}) async-start(), calls=%async_computation.2 | async-start | bytes 5898240 | tf_op jit(solution)/shard_map/all_gather | solution.py:100
  10.7 23.3 %copy-start.3 = (bf16[1,32,16,640]{3,2,1,0:T(8,128)(2,1)}, bf16[1,32,16,640]{3,2,1,0:T(8,128)(2,1)S(1)}, u32[]{:S(2)}) copy-start(bf16[1,32,16,640]{3,2,1,0:T(8,128)(2,1)S(1)} %fusion.35) | copy-start | bytes 1966084
  29.6 0.8 copy-start.4
  34.0 40.1 %copy-start.9 = (bf16[1,16,8,640]{3,2,1,0:T(8,128)(2,1)S(1)}, bf16[1,16,8,640]{3,2,1,0:T(8,128)(2,1)}, u32[]{:S(2)}) copy-start(bf16[1,16,8,640]{3,2,1,0:T(8,128)(2,1)} %param.14) | copy-start | bytes 491524
  34.1 22.6 %collective-permute-start = (bf16[1,16,16,1280]{3,2,1,0:T(8,128)(2,1)S(1)}, bf16[1,16,16,1280]{3,2,1,0:T(8,128)(2,1)S(1)}, u32[]{:S(2)}, u32[]{:S(2)}) collective-permute-start(bf16[1,16,16,1280]{3,2,1,0:T(8,128)(2,1)S(1)} %get-tuple-element.159), channel_id=1, source_target_pairs={{0,16},{16,32},{32,48},{48,64},{64,80},{80,96},{96,112},{1,17},{17... | collective-permute-start | bytes 1966088 | tf_op jit(solution)/shard_map/ppermute | solution.py:16
  37.7 27.8 %collective-permute-start.1 = (bf16[1,16,16,1280]{3,2,1,0:T(8,128)(2,1)S(1)}, bf16[1,16,16,1280]{3,2,1,0:T(8,128)(2,1)S(1)}, u32[]{:S(2)}, u32[]{:S(2)}) collective-permute-start(bf16[1,16,16,1280]{3,2,1,0:T(8,128)(2,1)S(1)} %get-tuple-element.160), channel_id=1, source_target_pairs={{16,0},{32,16},{48,32},{64,48},{80,64},{96,80},{112,96},{17,1},{33... | collective-permute-start | bytes 1966088 | tf_op jit(solution)/shard_map/ppermute | solution.py:19
  56.7 8.8 %copy-start.5 = (bf16[1,16,16,1280]{3,2,1,0:T(8,128)(2,1)}, bf16[1,16,16,1280]{3,2,1,0:T(8,128)(2,1)S(1)}, u32[]{:S(2)}) copy-start(bf16[1,16,16,1280]{3,2,1,0:T(8,128)(2,1)S(1)} %collective-permute-done) | copy-start | bytes 1966084
  65.5 1.8 copy-start.7
  67.3 9.3 %copy-start.14 = (f32[32,16]{0,1:T(8,128)S(1)}, f32[32,16]{0,1:T(8,128)}, u32[]{:S(2)}) copy-start(f32[32,16]{0,1:T(8,128)} %param.16) | copy-start | bytes 6148
  67.3 10.7 %copy-start.15 = (f32[32,16]{0,1:T(8,128)S(1)}, f32[32,16]{0,1:T(8,128)}, u32[]{:S(2)}) copy-start(f32[32,16]{0,1:T(8,128)} %param.15) | copy-start | bytes 6148
  67.3 89.1 %collective-permute-start.2 = (bf16[1,64,16,1280]{3,2,1,0:T(8,128)(2,1)}, bf16[1,64,16,1280]{3,2,1,0:T(8,128)(2,1)}, u32[]{:S(2)}, u32[]{:S(2)}) collective-permute-start(bf16[1,64,16,1280]{3,2,1,0:T(8,128)(2,1)} %pad_maximum_fusion.1), channel_id=1, source_target_pairs={{0,1},{1,2},{2,3},{3,4},{4,5},{5,6},{6,7},{7,8},{8,9},{9,10},{10,1... | collective-permute-start | bytes 7864328 | tf_op jit(solution)/shard_map/ppermute | solution.py:16
  71.3 85.1 %collective-permute-start.3 = (bf16[1,64,16,1280]{3,2,1,0:T(8,128)(2,1)}, bf16[1,64,16,1280]{3,2,1,0:T(8,128)(2,1)}, u32[]{:S(2)}, u32[]{:S(2)}) collective-permute-start(bf16[1,64,16,1280]{3,2,1,0:T(8,128)(2,1)} %pad_maximum_fusion.1), channel_id=1, source_target_pairs={{1,0},{2,1},{3,2},{4,3},{5,4},{6,5},{7,6},{8,7},{9,8},{10,9},{11,1... | collective-permute-start | bytes 7864328 | tf_op jit(solution)/shard_map/ppermute | solution.py:19
  76.6 79.8 %copy-start.6 = (bf16[1,16,16,1280]{3,2,1,0:T(8,128)(2,1)S(1)}, bf16[1,16,16,1280]{3,2,1,0:T(8,128)(2,1)}, u32[]{:S(2)}) copy-start(bf16[1,16,16,1280]{3,2,1,0:T(8,128)(2,1)} %copy-done.5) | copy-start | bytes 1966084
  79.4 77.1 %copy-start.8 = (bf16[1,16,16,1280]{3,2,1,0:T(8,128)(2,1)S(1)}, bf16[1,16,16,1280]{3,2,1,0:T(8,128)(2,1)}, u32[]{:S(2)}) copy-start(bf16[1,16,16,1280]{3,2,1,0:T(8,128)(2,1)} %copy-done.7) | copy-start | bytes 1966084
  163.7 3.7 copy-start.16
  163.7 3.7 copy-start.17
  283.4 103.0 %all-to-all-start.1 = ((bf16[1,1,8,64,640]{4,2,1,0,3:T(8,128)(2,1)}), bf16[1,1,8,64,640]{4,2,1,0,3:T(8,128)(2,1)S(1)}, u32[]{:S(2)}, u32[]{:S(2)}) async-start(bf16[1,1,8,64,640]{4,2,1,0,3:T(8,128)(2,1)} %copy.42), calls=%async_computation.1 | async-start | bytes 1310720 | tf_op jit(solution)/shard_map/all_to_all | solution.py:112
  386.4 2.6 copy-start.2
  386.4 2.6 copy-start.10
  386.4 2.6 copy-start.11
  386.4 2.6 copy-start.12
  386.4 2.6 copy-start.13
  386.6 6.4 %copy-start.1 = (bf16[640,640]{1,0:T(8,128)(2,1)S(1)}, bf16[640,640]{1,0:T(8,128)(2,1)}, u32[]{:S(2)}) copy-start(bf16[640,640]{1,0:T(8,128)(2,1)} %param.18) | copy-start | bytes 2457604
Sparse Core Ops, SparseCore 0:
  31.5 128.3 all-gather.1
where the time goes:
time: 402 us; the launch traced here: 400 us
  matrix products  150 us (37%)
  waiting for transfers between devices  98.1 us (24%)
  local copies, waits for them, and re-layouts  46.8 us (12%)
  other arithmetic  43.3 us (11%)
  blocking collectives  18.4 us (5%)
  starting transfers between devices  16.2 us (4%)
  between operations  13.7 us (3%)
  loops' own time  13.1 us (3%)
    ppermute x2, waiting for transfers between devices, padded(): lax.ppermute(lax.slice_in_dim(block, block.shape[dim] - width, None, axis...  89.3 us
    dot_general x20, matrix products, one_head(): return jnp.dot(weights, value_head, preferred_element_type=jnp.float32)  72.1 us
    dot_general x20, matrix products, one_head(): jnp.dot(query_head, key_head.T, preferred_element_type=jnp.float32) * factor  51.4 us
    reduce_sum x20, other arithmetic, one_head(): jnp.sum(raised, axis=1, keepdims=True)  29.2 us
    dot_general x4, matrix products, project(): jnp.dot(tensor, matrix, preferred_element_type=jnp.float32)  22.6 us
    all_to_all x1, blocking collectives, shards(): lax.all_to_all(to_phases(normed), 'phase', split_axis=0, concat_axis=3, t...  18.4 us
    another operation x2, loops' own time, attend(): stacked = lax.map(one_head, jnp.arange(HEADS, dtype=jnp.int32))  13.1 us
    dynamic_slice x20, local copies, waits for them, and re-layouts, attend(): stacked = lax.map(one_head, jnp.arange(HEADS, dtype=jnp.int32))  11.8 us
  transfers between devices with their start and end apart: 6, of which 3 were waited for; matrix products, arithmetic and copies ran while one was open for 30% of the time, Pallas kernels for 0%

commit v1 on v0

v1 whole, which is shorter than its diff:
```python
import functools

import jax
import jax.numpy as jnp
from jax import lax
from jax.experimental import pallas as pl
from jax.experimental.pallas import tpu as pltpu
from jax.sharding import PartitionSpec as P

HEADS = 10
HD = 64
C = 640
TOK = 512
CHUNK = 512
WIN = 3072
SUB = 4096
ROWS = 1024
AUG = 80
NEG = -1e30
SCALE = 0.125 * 1.4426950408889634
MESH = pl.DeviceIdType.MESH
BF = jnp.bfloat16
F32 = jnp.float32


def dot(a, b):
    return jnp.dot(a, b, preferred_element_type=F32)


def dot_nt(a, b):
    return lax.dot_general(a, b, (((1,), (1,)), ((), ())), preferred_element_type=F32)


def pipeline(count, scores, weigh):
    scores(0, 0)
    loops = (count - 1) // 2

    def body(i, carry):
        scores(2 * i + 1, 1)
        weigh(2 * i, 0)
        scores(2 * i + 2, 0)
        weigh(2 * i + 1, 1)
        return carry

    if loops:
        lax.fori_loop(0, loops, body, 0)
    if count % 2:
        weigh(count - 1, 0)
    else:
        scores(count - 1, 1)
        weigh(count - 2, 0)
        weigh(count - 1, 1)


def kernel(
    latent_ref, previous_ref, blend_ref, skip_ref, gain_ref, wq_ref, wk_ref, wv_ref, wo_ref,
    out_ref,
    wqt, wvt, nrm, halo_lr, halo_s, gat, qpad, kwin, vaug, acc, run_max, s_buf, s_max,
    wkd, wqd, wvd, qd, kd, vaug_d, acc_d, max_d, dil, ret, local,
    a2a_send, a2a_recv, halo_send, halo_recv, z_send, z_recv, c_send, c_recv, r_send, r_recv,
):
    t, p = lax.axis_index("tile"), lax.axis_index("phase")
    z, y_hi = t % 4, t // 4
    x, y_lo, core = p // 4, (p // 2) % 2, p % 2
    me = x * 4 + y_hi * 2 + y_lo

    def column(s, c):
        return ((s // 2) % 2 * 4 + z, s // 4 * 4 + s % 2 * 2 + c)

    up, down = ((t + 7) % 8, p), ((t + 1) % 8, p)
    left, right = (t, (p + 15) % 16), (t, (p + 1) % 16)
    z_next, z_prev = (y_hi * 4 + (z + 1) % 4, p), (y_hi * 4 + (z + 3) % 4, p)
    other = (t, p + 1 - 2 * core)

    barrier = pltpu.get_barrier_semaphore()
    for device in (up, down, left, right, z_next, z_prev):
        pl.semaphore_signal(barrier, inc=1, device_id=device, device_id_type=MESH)

    def greet(k, carry):
        pl.semaphore_signal(
            barrier, inc=1, device_id=column((me + k // 2) % 16, (core + k) % 2), device_id_type=MESH
        )
        return carry

    lax.fori_loop(1, 32, greet, 0)

    def order(shape, dim):
        r = lax.broadcasted_iota(jnp.int32, shape, dim)
        f, k = r // 32, r % 32
        return (4 * (k // 4) + f // 4) * 16 + 4 * (k % 4) + f % 4

    wide = latent_ref[...].astype(F32)
    average = jnp.mean(wide, axis=-1, keepdims=True)
    centred = wide - average
    variance = jnp.mean(centred * centred, axis=-1, keepdims=True)
    natural = (centred * lax.rsqrt(variance + 1e-5) * gain_ref[...]).astype(BF)
    pick = jnp.where(
        order((TOK, TOK), 0) == lax.broadcasted_iota(jnp.int32, (TOK, TOK), 1), 1.0, 0.0
    ).astype(BF)
    nrm[...] = dot(pick, natural).astype(BF).reshape(16, 32, C)

    pl.semaphore_wait(barrier, 37)

    def remote(src, dst, send, recv, device):
        return pltpu.make_async_remote_copy(
            src_ref=src, dst_ref=dst, send_sem=send, recv_sem=recv, device_id=device, device_id_type=MESH
        )

    def halo(i):
        if i < 2:
            return remote(nrm, halo_lr.at[i], halo_send.at[i], halo_recv.at[i], (right, left)[i])
        if i == 2:
            src, device = nrm.at[:, pl.ds(16, 16)], down
        elif i == 3:
            src, device = nrm.at[:, pl.ds(0, 16)], up
        else:
            src, device = halo_s.at[(i - 4) // 2], (right, left)[i % 2]
        return remote(src, halo_s.at[i - 2], halo_send.at[i], halo_recv.at[i], device)

    def exchange(k):
        to = (me + k) % 16
        return remote(
            nrm.at[to], gat.at[z, core, me], a2a_send.at[k], a2a_recv.at[k], column(to, core)
        )

    def exchanged(k):
        return remote(
            nrm.at[0], gat.at[z, core, (me + 16 - k) % 16], a2a_send.at[k], a2a_recv.at[k], column(me, core)
        )

    def ring(i):
        if i < 2:
            shard = gat.at[z, core]
        else:
            shard = gat.at[(z + (3, 1)[i - 2]) % 4, core, pl.ds(8 * (i - 2), 8)]
        return remote(shard, shard, z_send.at[i], z_recv.at[i], (z_next, z_prev)[i % 2])

    def ringed(i):
        if i < 2:
            shard = gat.at[(z + (3, 1)[i]) % 4, core]
        else:
            shard = gat.at[(z + 2) % 4, core, pl.ds(8 * (i - 2), 8)]
        return remote(shard, shard, z_send.at[i], z_recv.at[i], (z_next, z_prev)[i % 2])

    def across(i):
        shard = gat.at[(z + (0, 3, 1, 2)[i]) % 4, core]
        return remote(shard, shard, c_send.at[i], c_recv.at[i], other)

    def crossed(i):
        shard = gat.at[(z + (0, 3, 1, 2)[i]) % 4, 1 - core]
        return remote(shard, shard, c_send.at[i], c_recv.at[i], other)

    def each(first, last, act):
        def body(k, carry):
            act(k)
            return carry

        lax.fori_loop(first, last, body, 0)

    halo(2).start()
    halo(3).start()
    each(1, 16, lambda k: exchange(k).start())
    halo(0).start()
    halo(1).start()
    gat[z, core, me] = nrm[me]

    wqt[...] = wq_ref[...].T
    wvt[...] = wv_ref[...].T
    vaug[:, HD:, :] = jnp.ones((HEADS, AUG - HD, WIN), BF)
    vaug_d[:, HD:, :] = jnp.ones((5, AUG - HD, SUB), BF)

    own = nrm[...].reshape(TOK, C)
    queries = dot_nt(wqt[...], own).astype(BF)
    zeros = jnp.zeros((HD, TOK), BF)
    for j in range(5):
        first, second = queries[j * 128 : j * 128 + HD], queries[j * 128 + HD : j * 128 + 128]
        qpad[j, :HD, :TOK] = first
        qpad[j, HD:, :TOK] = zeros
        qpad[j, :HD, TOK:] = zeros
        qpad[j, HD:, TOK:] = second

    def window(tokens, chunk):
        at = pl.multiple_of(chunk * CHUNK, CHUNK)
        kwin[pl.ds(at, CHUNK), :] = dot(tokens, wk_ref[...]).astype(BF)
        vaug[:, :HD, pl.ds(at, CHUNK)] = dot_nt(wvt[...], tokens).astype(BF).reshape(HEADS, HD, CHUNK)

    top, bottom, west, east = t == 0, t == 7, p == 0, p == 15

    def penalties(chunk):
        outside_a = (
            (top & ((chunk == 3) | (chunk == 4)))
            | (bottom & (chunk == 5))
            | (west & ((chunk == 1) | (chunk == 4) | (chunk == 5)))
            | (east & (chunk == 2))
        )
        outside_b = (
            (bottom & ((chunk == 3) | (chunk == 5)))
            | (top & (chunk == 4))
            | (west & (chunk == 1))
            | (east & ((chunk == 2) | (chunk == 4) | (chunk == 5)))
        )
        return jnp.where(outside_a, -NEG, 0.0), jnp.where(outside_b, -NEG, 0.0)

    half = CHUNK // 2

    def attend_window(base, chunks):
        def place(i):
            return i // chunks, base + i % chunks

        def scores(i, slot):
            pair, chunk = place(i)
            s = dot(
                kwin[pl.ds(pl.multiple_of(chunk * CHUNK, CHUNK), CHUNK), pl.ds(pl.multiple_of(pair * 128, 128), 128)],
                qpad[pair],
            )
            s_buf[slot] = s
            pen_a, pen_b = penalties(chunk)
            s_max[slot, 0:1, :] = jnp.maximum(
                jnp.max(s[:half], axis=0, keepdims=True) - pen_a, jnp.max(s[half:], axis=0, keepdims=True) - pen_b
            )

        def weigh(i, slot):
            pair, chunk = place(i)
            pen_a, pen_b = penalties(chunk)
            if base == 0:
                new = s_max[slot, 0:1, :]
            else:
                old = run_max[pair, 0:1, :]
                new = jnp.maximum(old, s_max[slot, 0:1, :])
                fade = jnp.exp2((old - new) * SCALE)
            run_max[pair, 0:1, :] = new
            s = s_buf[slot]
            weights = jnp.concatenate(
                [
                    jnp.exp2(((s[:half] - (new + pen_a)) * SCALE).astype(BF)),
                    jnp.exp2(((s[half:] - (new + pen_b)) * SCALE).astype(BF)),
                ],
                axis=0,
            )
            at = pl.multiple_of(chunk * CHUNK, CHUNK)
            for b in range(2):
                h = 2 * pair + b
                cols = slice(b * TOK, (b + 1) * TOK)
                part = dot(vaug[h, :, pl.ds(at, CHUNK)], weights[:, cols])
                if base:
                    part = acc[h] * fade[:, cols] + part
                acc[h] = part

        pipeline(5 * chunks, scores, weigh)

    window(own, 0)
    attend_window(0, 1)

    each(1, 16, lambda k: exchanged(k).wait_recv())
    for i in range(2):
        ring(i).start()
    across(0).start()
    for i in (2, 3):
        halo(i).wait_recv()
    for i in range(4, 8):
        halo(i).start()
    for i in (0, 1):
        halo(i).wait_recv()
    each(1, 3, lambda c: window(halo_lr[c - 1].reshape(CHUNK, C), c))
    attend_window(1, 2)

    for i in (0, 1):
        ringed(i).wait_recv()
        ring(2 + i).start()
        across(1 + i).start()
    for i in range(4, 8):
        halo(i).wait_recv()
    each(3, 6, lambda c: window(halo_s[pl.ds(2 * (c - 3), 2)].reshape(CHUNK, C), c))
    attend_window(3, 3)

    for i in (2, 3):
        ringed(i).wait_recv()
    across(3).start()

    for j in range(5):
        both = [acc[2 * j + b, :HD] / acc[2 * j + b, HD : HD + 1] for b in range(2)]
        local[:, j * 128 : (j + 1) * 128] = jnp.concatenate(both, axis=0).T

    wkd[:, :256] = wk_ref[:, pl.ds(pl.multiple_of(core * 384, 128), 256)]
    wkd[:, 256:] = wk_ref[:, 256:384]
    wqd[:256] = wqt[pl.ds(pl.multiple_of(core * 384, 128), 256), :]
    wqd[256:] = wqt[pl.ds(pl.multiple_of(256 + core * 64, 64), HD), :]
    wvd[:256] = wvt[pl.ds(pl.multiple_of(core * 384, 128), 256), :]
    wvd[256:] = wvt[pl.ds(pl.multiple_of(256 + core * 64, 64), HD), :]
    qd[...] = jnp.zeros_like(qd)

    for c in range(2):
        if c == 0:
            for i in range(4):
                crossed(i).wait_recv()
        tokens = gat[z, c].reshape(CHUNK, C)
        part = dot_nt(wqd[...], tokens).astype(BF)
        cols = slice(c * CHUNK, (c + 1) * CHUNK)
        for i in range(4):
            qd[i, i % 2 * HD : i % 2 * HD + HD, cols] = part[i * HD : (i + 1) * HD]
        qd[4, pl.ds(pl.multiple_of(core * HD, HD), HD), cols] = part[256:]

    def sub_chunk(g):
        tokens = gat[g // 2, g % 2].reshape(CHUNK, C)
        at = pl.multiple_of(g * CHUNK, CHUNK)
        keys = dot(tokens, wkd[...]).astype(BF)
        for j in range(3):
            kd[j, pl.ds(at, CHUNK), :] = keys[:, j * 128 : (j + 1) * 128]
        vaug_d[:, :HD, pl.ds(at, CHUNK)] = dot_nt(wvd[...], tokens).astype(BF).reshape(5, HD, CHUNK)

    each(0, 8, sub_chunk)

    def give(j, k):
        s, c = (me + k // 2) % 16, (core + k) % 2
        return remote(
            dil.at[j, c * 16 + s], ret.at[core, j, me], r_send.at[j, k], r_recv.at[j, k], column(s, c)
        )

    def given(j, k):
        s, c = (me + 16 - k // 2) % 16, (core + k) % 2
        return remote(dil.at[j, 0], ret.at[c, j, s], r_send.at[j, k], r_recv.at[j, k], column(me, core))

    def attend_sub(first, heads):
        def scores(i, slot):
            h, g = first + i // 8, i % 8
            s = dot(kd[h // 2, pl.ds(pl.multiple_of(g * CHUNK, CHUNK), CHUNK), :], qd[h])
            s_buf[slot] = s
            s_max[slot, 0:1, :] = jnp.max(s, axis=0, keepdims=True)

        def weigh(i, slot):
            h, g = first + i // 8, i % 8
            old = max_d[h, 0:1, :]
            new = jnp.maximum(old, s_max[slot, 0:1, :])
            fade = jnp.exp2((old - new) * SCALE)
            max_d[h, 0:1, :] = new
            weights = jnp.exp2(((s_buf[slot] - new) * SCALE).astype(BF))
            values = vaug_d[h, :, pl.ds(pl.multiple_of(g * CHUNK, CHUNK), CHUNK)]
            for b in range(2):
                cols = slice(b * TOK, (b + 1) * TOK)
                acc_d[h, :, cols] = acc_d[h, :, cols] * fade[:, cols] + dot(values, weights[:, cols])

        pipeline(8 * heads, scores, weigh)

    max_d[...] = jnp.full_like(max_d, NEG)
    acc_d[...] = jnp.zeros_like(acc_d)
    for j in range(3):
        attend_sub(2 * j, 2 if j < 2 else 1)
        if j < 2:
            both = [acc_d[2 * j + b, :HD] / acc_d[2 * j + b, HD : HD + 1] for b in range(2)]
        else:
            only = acc_d[4, :HD] / acc_d[4, HD : HD + 1]
            both = [jnp.where(core == b, only, 0.0) for b in range(2)]
        dil[j] = jnp.concatenate(both, axis=0).T.astype(BF).reshape(32, 32, 128)
        each(1, 32, lambda k: give(j, k).start())
        ret[core, j, me] = dil[j, core * 16 + me]

    def position(ref, natural_of):
        rows = jnp.where(
            natural_of((TOK, 32), 0) // 16 == lax.broadcasted_iota(jnp.int32, (TOK, 32), 1), 1.0, 0.0
        )
        spread = jnp.dot(rows, ref[...], preferred_element_type=F32, precision=lax.Precision.HIGHEST)
        here = natural_of((TOK, 16), 0) % 16 == lax.broadcasted_iota(jnp.int32, (TOK, 16), 1)
        return jnp.sum(jnp.where(here, spread, 0.0), axis=1, keepdims=True)

    def plain(shape, dim):
        return lax.broadcasted_iota(jnp.int32, shape, dim)

    mixing = position(blend_ref, order)
    keeping = position(skip_ref, plain)
    token = plain((TOK, 128), 0)
    source = token // 32 * 8 + token % 16 // 2
    repeat = jnp.where(source == lax.broadcasted_iota(jnp.int32, (TOK, 128), 1), 1.0, 0.0).astype(BF)
    upsampled = dot(repeat, previous_ref[...])
    place_back = jnp.where(
        order((TOK, TOK), 1) == lax.broadcasted_iota(jnp.int32, (TOK, TOK), 0), 1.0, 0.0
    ).astype(BF)

    for j in range(3):
        each(1, 32, lambda k: given(j, k).wait_recv())

    columns = []
    for pair in range(5):
        if pair == 2:
            dilated = ret[0, 2].astype(F32) + ret[1, 2].astype(F32)
        else:
            dilated = ret[pair // 3, pair % 3].astype(F32)
        dilated = dilated.reshape(TOK, 128)
        columns.append(
            ((1.0 - mixing) * local[:, pair * 128 : (pair + 1) * 128] + mixing * dilated).astype(BF)
        )
    mixed = dot(place_back, jnp.concatenate(columns, axis=1)).astype(BF)
    attention = dot(mixed, wo_ref[...])
    out_ref[...] = (
        (1.0 - keeping) * (latent_ref[...].astype(F32) + attention) + keeping * upsampled
    ).astype(BF)

    each(1, 16, lambda k: exchange(k).wait_send())
    for i in range(8):
        halo(i).wait_send()
    for i in range(4):
        ring(i).wait_send()
        across(i).wait_send()
    for j in range(3):
        each(1, 32, lambda k: give(j, k).wait_send())


def shards(latent, previous, blend_weight, skip_weight, norm_gain, w_query, w_key, w_value, w_out):
    vmem = pltpu.VMEM
    dma = pltpu.SemaphoreType.DMA
    result = pl.pallas_call(
        kernel,
        out_shape=jax.ShapeDtypeStruct((TOK, C), BF),
        in_specs=[pl.BlockSpec(memory_space=pltpu.VMEM)] * 9,
        out_specs=pl.BlockSpec(memory_space=pltpu.VMEM),
        scratch_shapes=[
            vmem((C, C), BF),
            vmem((C, C), BF),
            vmem((16, 32, C), BF),
            vmem((2, 16, 32, C), BF),
            vmem((6, 16, 16, C), BF),
            vmem((4, 2, 16, 32, C), BF),
            vmem((5, 128, ROWS), BF),
            vmem((WIN, C), BF),
            vmem((HEADS, AUG, WIN), BF),
            vmem((HEADS, AUG, TOK), F32),
            vmem((5, 8, ROWS), F32),
            vmem((2, CHUNK, ROWS), F32),
            vmem((2, 8, ROWS), F32),
            vmem((C, 384), BF),
            vmem((320, C), BF),
            vmem((320, C), BF),
            vmem((5, 128, ROWS), BF),
            vmem((3, SUB, 128), BF),
            vmem((5, AUG, SUB), BF),
            vmem((5, AUG, ROWS), F32),
            vmem((5, 8, ROWS), F32),
            vmem((3, 32, 32, 128), BF),
            vmem((2, 3, 16, 32, 128), BF),
            vmem((TOK, C), F32),
            dma((16,)), dma((16,)), dma((8,)), dma((8,)), dma((4,)), dma((4,)), dma((4,)), dma((4,)),
            dma((3, 32)), dma((3, 32)),
        ],
        compiler_params=pltpu.CompilerParams(
            collective_id=0, has_side_effects=True, vmem_limit_bytes=60 * 2**20
        ),
    )(
        latent.reshape(TOK, C), previous.reshape(128, C), blend_weight, skip_weight,
        norm_gain.reshape(1, C), w_query, w_key, w_value, w_out,
    )
    return result.reshape(latent.shape)


def solution(mesh):
    return jax.shard_map(
        shards,
        mesh=mesh,
        in_specs=(
            P(None, "tile", "phase", None),
            P(None, "tile", "phase", None),
            P("tile", "phase"),
            P("tile", "phase"),
            P(),
            P(),
            P(),
            P(),
            P(),
        ),
        out_specs=P(None, "tile", "phase", None),
        check_vma=False,
    )
```

time: 402 us -> 124 us (0.31)
  matrix products: 150 us -> 0 us
  Pallas kernels: 0 us -> 119 us
  waiting for transfers between devices: 98.1 us -> 0 us
  other arithmetic: 43.3 us -> 0 us
  local copies, waits for them, and re-layouts: 46.8 us -> 4.64 us
  blocking collectives: 18.4 us -> 0 us
  starting transfers between devices: 16.2 us -> 0 us
  between operations: 13.7 us -> 0.01 us
  loops' own time: 13.1 us -> 0 us
    dot_general x45 -> x0, matrix products: 150 us -> none  [the longest x20 72.1 us: one_head(): return jnp.dot(weights, value_head, preferred_element_type=jnp.float32)]
    pallas_call x0 -> x1, Pallas kernels: none -> 119 us  [shards(): pl.pallas_call(kernel, out_shape=jax.ShapeDtypeStruct((TOK, C), BF), in_s...]
    ppermute x4 -> x0, waiting for transfers between devices: 98.1 us -> none  [the longest x2 89.3 us: padded(): lax.ppermute(lax.slice_in_dim(block, block.shape[dim] - width, None, axis...]
    reduce_sum x22 -> x0, other arithmetic: 31.9 us -> none  [the longest x20 29.2 us: one_head(): jnp.sum(raised, axis=1, keepdims=True)]
    all_to_all x1 -> x0, blocking collectives: 18.4 us -> none  [shards(): lax.all_to_all(to_phases(normed), 'phase', split_axis=0, concat_axis=3, t...]
    another operation x2 -> x0, loops' own time: 13.1 us -> none  [attend(): stacked = lax.map(one_head, jnp.arange(HEADS, dtype=jnp.int32))]
    slice x3 -> x0, local copies, waits for them, and re-layouts: 12.6 us -> none  [the longest x1 8.79 us: per_phase(): couple[1][:, channels:]]
    dynamic_slice x20 -> x0, local copies, waits for them, and re-layouts: 11.8 us -> none  [attend(): stacked = lax.map(one_head, jnp.arange(HEADS, dtype=jnp.int32))]
  transfers between devices with their start and end apart: 6 -> 0, of which waited for: 3 -> 0; matrix products, arithmetic and copies ran while one was open for 30% -> 0% of each run, Pallas kernels for 0% -> 0%
where the time goes in v1:
time: 124 us
  Pallas kernels  119 us (96%)
  local copies, waits for them, and re-layouts  4.64 us (4%)
    pallas_call x1, Pallas kernels, shards(): pl.pallas_call(kernel, out_shape=jax.ShapeDtypeStruct((TOK, C), BF), in_s...  119 us
    unnamed x7, local copies, waits for them, and re-layouts  3.35 us

profile of v1, /device:TPU:1, one launch (start us, length us, event | category | flops | bytes accessed | tf_op | source)
XLA Modules:
  0.0 123.7 jit_solution(12652029144749512844)
XLA Ops:
  0.0 0.0 copy-start
  0.0 1.3 %reshape.14.gain_ref = f32[1,640]{1,0:T(1,128)} reshape(f32[640]{0:T(1024)} %param.13) | data formatting | bytes 5120 | tf_op jit(solution)/shard_map/reshape | solution.py:448
  1.3 0.0 copy-done
  1.3 0.0 copy-start.1
  1.3 0.7 copy.10.blend_ref
  2.0 0.0 copy-done.1
  2.0 0.7 copy.11.skip_ref
  2.7 119.0 %shard_map.91 = bf16[512,640]{1,0:T(8,128)(2,1)} custom-call(bf16[512,640]{1,0:T(8,128)(2,1)} %bitcast.4, bf16[128,640]{1,0:T(8,128)(2,1)} %bitcast.5, f32[32,16]{1,0:T(8,128)} %copy.10.blend_ref, f32[32,16]{1,0:T(8,128)} %copy.11.skip_ref, f32[1,640]{1,0:T(1,128)} %reshape.14.gain_ref, bf16[640,640]{1,0:T(8,128)(2,1)} %wq_ref.1, bf16[640,640]{1,0:T(8,128)(2,1)} %wk_ref.1, ...), custom_call_target="tpu_custom_call" | custom-call | tf_op jit(solution)/shard_map/pallas_call | solution.py:410
  121.7 2.0 %copy.13 = bf16[1,32,16,640]{3,2,1,0:T(8,128)(2,1)} copy(bf16[1,32,16,640]{3,2,1,0:T(8,128)(2,1)} %bitcast.3) | data formatting | bytes 1310720
Async XLA Ops:
  0.0 1.3 %copy-start = (f32[32,16]{0,1:T(8,128)S(1)}, f32[32,16]{0,1:T(8,128)}, u32[]{:S(2)}) copy-start(f32[32,16]{0,1:T(8,128)} %param.11) | copy-start | bytes 6148
  1.3 0.7 copy-start.1

commit v2 on v1

--- a/solution.py
+++ b/solution.py
@@ -68,12 +68,12 @@
         return ((s // 2) % 2 * 4 + z, s // 4 * 4 + s % 2 * 2 + c)
 
     up, down = ((t + 7) % 8, p), ((t + 1) % 8, p)
-    left, right = (t, (p + 15) % 16), (t, (p + 1) % 16)
+    far = (t, (p + 15 + 2 * core) % 16)
     z_next, z_prev = (y_hi * 4 + (z + 1) % 4, p), (y_hi * 4 + (z + 3) % 4, p)
     other = (t, p + 1 - 2 * core)
 
     barrier = pltpu.get_barrier_semaphore()
-    for device in (up, down, left, right, z_next, z_prev):
+    for device in (up, down, far, z_next, z_prev):
         pl.semaphore_signal(barrier, inc=1, device_id=device, device_id_type=MESH)
 
     def greet(k, carry):
@@ -93,13 +93,13 @@
     average = jnp.mean(wide, axis=-1, keepdims=True)
     centred = wide - average
     variance = jnp.mean(centred * centred, axis=-1, keepdims=True)
-    natural = (centred * lax.rsqrt(variance + 1e-5) * gain_ref[...]).astype(BF)
+    natural = (centred * lax.rsqrt(variance + 1e-5) * gain_ref[...][None, :]).astype(BF)
     pick = jnp.where(
         order((TOK, TOK), 0) == lax.broadcasted_iota(jnp.int32, (TOK, TOK), 1), 1.0, 0.0
     ).astype(BF)
     nrm[...] = dot(pick, natural).astype(BF).reshape(16, 32, C)
 
-    pl.semaphore_wait(barrier, 37)
+    pl.semaphore_wait(barrier, 36)
 
     def remote(src, dst, send, recv, device):
         return pltpu.make_async_remote_copy(
@@ -108,13 +108,13 @@
 
     def halo(i):
         if i < 2:
-            return remote(nrm, halo_lr.at[i], halo_send.at[i], halo_recv.at[i], (right, left)[i])
+            return remote(nrm, halo_lr.at[i], halo_send.at[i], halo_recv.at[i], (other, far)[i])
         if i == 2:
             src, device = nrm.at[:, pl.ds(16, 16)], down
         elif i == 3:
             src, device = nrm.at[:, pl.ds(0, 16)], up
         else:
-            src, device = halo_s.at[(i - 4) // 2], (right, left)[i % 2]
+            src, device = halo_s.at[i % 2], (other, far)[(i - 4) // 2]
         return remote(src, halo_s.at[i - 2], halo_send.at[i], halo_recv.at[i], device)
 
     def exchange(k):
@@ -161,7 +161,6 @@
     halo(3).start()
     each(1, 16, lambda k: exchange(k).start())
     halo(0).start()
-    halo(1).start()
     gat[z, core, me] = nrm[me]
 
     wqt[...] = wq_ref[...].T
@@ -184,22 +183,16 @@
         kwin[pl.ds(at, CHUNK), :] = dot(tokens, wk_ref[...]).astype(BF)
         vaug[:, :HD, pl.ds(at, CHUNK)] = dot_nt(wvt[...], tokens).astype(BF).reshape(HEADS, HD, CHUNK)
 
-    top, bottom, west, east = t == 0, t == 7, p == 0, p == 15
+    top, bottom = t == 0, t == 7
+    edge = ((core == 0) & (p == 0)) | ((core == 1) & (p == 15))
 
     def penalties(chunk):
-        outside_a = (
-            (top & ((chunk == 3) | (chunk == 4)))
-            | (bottom & (chunk == 5))
-            | (west & ((chunk == 1) | (chunk == 4) | (chunk == 5)))
-            | (east & (chunk == 2))
-        )
-        outside_b = (
-            (bottom & ((chunk == 3) | (chunk == 5)))
-            | (top & (chunk == 4))
-            | (west & (chunk == 1))
-            | (east & ((chunk == 2) | (chunk == 4) | (chunk == 5)))
-        )
-        return jnp.where(outside_a, -NEG, 0.0), jnp.where(outside_b, -NEG, 0.0)
+        corner = (chunk == 2) | (chunk == 3) | (chunk == 5)
+        beyond = edge & (chunk >= 4)
+        return (
+            jnp.where((top & corner) | beyond, -NEG, 0.0),
+            jnp.where((bottom & corner) | beyond, -NEG, 0.0),
+        )
 
     half = CHUNK // 2
 
@@ -250,36 +243,24 @@
 
     window(own, 0)
     attend_window(0, 1)
+    halo(0).wait_recv()
+    window(halo_lr[0].reshape(CHUNK, C), 1)
+    attend_window(1, 1)
 
     each(1, 16, lambda k: exchanged(k).wait_recv())
     for i in range(2):
         ring(i).start()
     across(0).start()
+    halo(1).start()
     for i in (2, 3):
         halo(i).wait_recv()
     for i in range(4, 8):
         halo(i).start()
-    for i in (0, 1):
+    window(halo_s[:2].reshape(CHUNK, C), 2)
+    for i in (4, 5):
         halo(i).wait_recv()
-    each(1, 3, lambda c: window(halo_lr[c - 1].reshape(CHUNK, C), c))
-    attend_window(1, 2)
-
-    for i in (0, 1):
-        ringed(i).wait_recv()
-        ring(2 + i).start()
-        across(1 + i).start()
-    for i in range(4, 8):
-        halo(i).wait_recv()
-    each(3, 6, lambda c: window(halo_s[pl.ds(2 * (c - 3), 2)].reshape(CHUNK, C), c))
-    attend_window(3, 3)
-
-    for i in (2, 3):
-        ringed(i).wait_recv()
-    across(3).start()
-
-    for j in range(5):
-        both = [acc[2 * j + b, :HD] / acc[2 * j + b, HD : HD + 1] for b in range(2)]
-        local[:, j * 128 : (j + 1) * 128] = jnp.concatenate(both, axis=0).T
+    window(halo_s[2:4].reshape(CHUNK, C), 3)
+    attend_window(2, 2)
 
     wkd[:, :256] = wk_ref[:, pl.ds(pl.multiple_of(core * 384, 128), 256)]
     wkd[:, 256:] = wk_ref[:, 256:384]
@@ -288,11 +269,11 @@
     wvd[:256] = wvt[pl.ds(pl.multiple_of(core * 384, 128), 256), :]
     wvd[256:] = wvt[pl.ds(pl.multiple_of(256 + core * 64, 64), HD), :]
     qd[...] = jnp.zeros_like(qd)
-
+    max_d[...] = jnp.full_like(max_d, NEG)
+    acc_d[...] = jnp.zeros_like(acc_d)
+
+    crossed(0).wait_recv()
     for c in range(2):
-        if c == 0:
-            for i in range(4):
-                crossed(i).wait_recv()
         tokens = gat[z, c].reshape(CHUNK, C)
         part = dot_nt(wqd[...], tokens).astype(BF)
         cols = slice(c * CHUNK, (c + 1) * CHUNK)
@@ -301,15 +282,15 @@
         qd[4, pl.ds(pl.multiple_of(core * HD, HD), HD), cols] = part[256:]
 
     def sub_chunk(g):
-        tokens = gat[g // 2, g % 2].reshape(CHUNK, C)
+        plane = jnp.where(g < 2, 0, jnp.where(g > 5, 2, jnp.where(g % 2 == 0, 3, 1)))
+        own_core = (g == 0) | (g == 2) | (g == 3) | (g == 6)
+        tokens = gat[(z + plane) % 4, jnp.where(own_core, core, 1 - core)].reshape(CHUNK, C)
         at = pl.multiple_of(g * CHUNK, CHUNK)
         keys = dot(tokens, wkd[...]).astype(BF)
         for j in range(3):
             kd[j, pl.ds(at, CHUNK), :] = keys[:, j * 128 : (j + 1) * 128]
         vaug_d[:, :HD, pl.ds(at, CHUNK)] = dot_nt(wvd[...], tokens).astype(BF).reshape(5, HD, CHUNK)
 
-    each(0, 8, sub_chunk)
-
     def give(j, k):
         s, c = (me + k // 2) % 16, (core + k) % 2
         return remote(
@@ -320,15 +301,18 @@
         s, c = (me + 16 - k // 2) % 16, (core + k) % 2
         return remote(dil.at[j, 0], ret.at[c, j, s], r_send.at[j, k], r_recv.at[j, k], column(me, core))
 
-    def attend_sub(first, heads):
+    def attend_sub(first, heads, base, chunks):
+        def place(i):
+            return first + i // chunks, base + i % chunks
+
         def scores(i, slot):
-            h, g = first + i // 8, i % 8
+            h, g = place(i)
             s = dot(kd[h // 2, pl.ds(pl.multiple_of(g * CHUNK, CHUNK), CHUNK), :], qd[h])
             s_buf[slot] = s
             s_max[slot, 0:1, :] = jnp.max(s, axis=0, keepdims=True)
 
         def weigh(i, slot):
-            h, g = first + i // 8, i % 8
+            h, g = place(i)
             old = max_d[h, 0:1, :]
             new = jnp.maximum(old, s_max[slot, 0:1, :])
             fade = jnp.exp2((old - new) * SCALE)
@@ -339,12 +323,39 @@
                 cols = slice(b * TOK, (b + 1) * TOK)
                 acc_d[h, :, cols] = acc_d[h, :, cols] * fade[:, cols] + dot(values, weights[:, cols])
 
-        pipeline(8 * heads, scores, weigh)
-
-    max_d[...] = jnp.full_like(max_d, NEG)
-    acc_d[...] = jnp.zeros_like(acc_d)
+        pipeline(chunks * heads, scores, weigh)
+
+    each(0, 2, sub_chunk)
+    attend_sub(0, 5, 0, 2)
+
+    for i in (0, 1):
+        ringed(i).wait_recv()
+        ring(2 + i).start()
+        across(1 + i).start()
+    each(2, 4, sub_chunk)
+    attend_sub(0, 5, 2, 2)
+
+    halo(1).wait_recv()
+    window(halo_lr[1].reshape(CHUNK, C), 4)
+    attend_window(4, 1)
+    for i in (2, 3):
+        ringed(i).wait_recv()
+    across(3).start()
+    for i in (6, 7):
+        halo(i).wait_recv()
+    window(halo_s[4:].reshape(CHUNK, C), 5)
+    attend_window(5, 1)
+    for j in range(5):
+        both = [acc[2 * j + b, :HD] / acc[2 * j + b, HD : HD + 1] for b in range(2)]
+        local[:, j * 128 : (j + 1) * 128] = jnp.concatenate(both, axis=0).T
+
+    for i in (1, 2):
+        crossed(i).wait_recv()
+    each(4, 7, sub_chunk)
+    crossed(3).wait_recv()
+    sub_chunk(7)
     for j in range(3):
-        attend_sub(2 * j, 2 if j < 2 else 1)
+        attend_sub(2 * j, 2 if j < 2 else 1, 4, 4)
         if j < 2:
             both = [acc_d[2 * j + b, :HD] / acc_d[2 * j + b, HD : HD + 1] for b in range(2)]
         else:
@@ -355,11 +366,11 @@
         ret[core, j, me] = dil[j, core * 16 + me]
 
     def position(ref, natural_of):
-        rows = jnp.where(
-            natural_of((TOK, 32), 0) // 16 == lax.broadcasted_iota(jnp.int32, (TOK, 32), 1), 1.0, 0.0
-        )
-        spread = jnp.dot(rows, ref[...], preferred_element_type=F32, precision=lax.Precision.HIGHEST)
-        here = natural_of((TOK, 16), 0) % 16 == lax.broadcasted_iota(jnp.int32, (TOK, 16), 1)
+        cols = jnp.where(
+            natural_of((TOK, 16), 0) % 16 == lax.broadcasted_iota(jnp.int32, (TOK, 16), 1), 1.0, 0.0
+        )
+        spread = jnp.dot(cols, ref[...], preferred_element_type=F32, precision=lax.Precision.HIGHEST)
+        here = natural_of((TOK, 32), 0) // 16 == lax.broadcasted_iota(jnp.int32, (TOK, 32), 1)
         return jnp.sum(jnp.where(here, spread, 0.0), axis=1, keepdims=True)
 
     def plain(shape, dim):
@@ -444,8 +455,8 @@
             collective_id=0, has_side_effects=True, vmem_limit_bytes=60 * 2**20
         ),
     )(
-        latent.reshape(TOK, C), previous.reshape(128, C), blend_weight, skip_weight,
-        norm_gain.reshape(1, C), w_query, w_key, w_value, w_out,
+        latent.reshape(TOK, C), previous.reshape(128, C), blend_weight.T, skip_weight.T,
+        norm_gain, w_query, w_key, w_value, w_out,
     )
     return result.reshape(latent.shape)
 

time: 124 us -> 109 us (0.88)
  Pallas kernels: 119 us -> 107 us
  local copies, waits for them, and re-layouts: 4.64 us -> 1.98 us
    pallas_call x1, Pallas kernels: 119 us -> 107 us  [shards(): pl.pallas_call(kernel, out_shape=jax.ShapeDtypeStruct((TOK, C), BF), in_s...]
    unnamed x7 -> x1, local copies, waits for them, and re-layouts: 3.35 us -> 1.98 us
    reshape x1 -> x0, local copies, waits for them, and re-layouts: 1.29 us -> none  [shards(): norm_gain.reshape(1, C)]
where the time goes in v2:
time: 109 us
  Pallas kernels  107 us (98%)
  local copies, waits for them, and re-layouts  1.98 us (2%)
    pallas_call x1, Pallas kernels, shards(): pl.pallas_call(kernel, out_shape=jax.ShapeDtypeStruct((TOK, C), BF), in_s...  107 us

profile of v2, /device:TPU:1, one launch (start us, length us, event | category | flops | bytes accessed | tf_op | source)
XLA Modules:
  0.0 108.8 jit_solution(12976981583542484015)
XLA Ops:
  0.0 106.8 %shard_map.91 = bf16[512,640]{1,0:T(8,128)(2,1)} custom-call(bf16[512,640]{1,0:T(8,128)(2,1)} %bitcast.6, bf16[128,640]{1,0:T(8,128)(2,1)} %bitcast.7, f32[16,32]{1,0:T(8,128)} %bitcast.8, f32[16,32]{1,0:T(8,128)} %bitcast.9, f32[640]{0:T(1024)} %gain_ref.1, bf16[640,640]{1,0:T(8,128)(2,1)} %wq_ref.1, bf16[640,640]{1,0:T(8,128)(2,1)} %wk_ref.1, ...), custom_call_target="tpu_custom_call" | custom-call | tf_op jit(solution)/shard_map/pallas_call | solution.py:421
  106.8 2.0 %copy.11 = bf16[1,32,16,640]{3,2,1,0:T(8,128)(2,1)} copy(bf16[1,32,16,640]{3,2,1,0:T(8,128)(2,1)} %bitcast.5) | data formatting | bytes 1310720

commit v3 on v2

--- a/solution.py
+++ b/solution.py
@@ -117,6 +117,34 @@
             src, device = halo_s.at[i % 2], (other, far)[(i - 4) // 2]
         return remote(src, halo_s.at[i - 2], halo_send.at[i], halo_recv.at[i], device)
 
+    edge = ((core == 0) & (p == 0)) | ((core == 1) & (p == 15))
+    above, below, beside = t > 0, t < 7, jnp.logical_not(edge)
+    sends = (None, beside, below, above, above, below, above & beside, below & beside)
+    receives = (None, beside, above, below, above, below, above & beside, below & beside)
+
+    def when(condition, act):
+        if condition is None:
+            act()
+        else:
+            pl.when(condition)(act)
+
+    def halo_start(i):
+        when(sends[i], lambda: halo(i).start())
+
+    def halo_sent(i):
+        when(sends[i], lambda: halo(i).wait_send())
+
+    def halo_here(i):
+        when(receives[i], lambda: halo(i).wait_recv())
+        if receives[i] is not None:
+
+            @pl.when(jnp.logical_not(receives[i]))
+            def _():
+                if i < 2:
+                    halo_lr[i] = jnp.zeros((16, 32, C), BF)
+                else:
+                    halo_s[i - 2] = jnp.zeros((16, 16, C), BF)
+
     def exchange(k):
         to = (me + k) % 16
         return remote(
@@ -157,10 +185,10 @@
 
         lax.fori_loop(first, last, body, 0)
 
-    halo(2).start()
-    halo(3).start()
+    halo_start(2)
+    halo_start(3)
     each(1, 16, lambda k: exchange(k).start())
-    halo(0).start()
+    halo_start(0)
     gat[z, core, me] = nrm[me]
 
     wqt[...] = wq_ref[...].T
@@ -184,7 +212,6 @@
         vaug[:, :HD, pl.ds(at, CHUNK)] = dot_nt(wvt[...], tokens).astype(BF).reshape(HEADS, HD, CHUNK)
 
     top, bottom = t == 0, t == 7
-    edge = ((core == 0) & (p == 0)) | ((core == 1) & (p == 15))
 
     def penalties(chunk):
         corner = (chunk == 2) | (chunk == 3) | (chunk == 5)
@@ -243,7 +270,7 @@
 
     window(own, 0)
     attend_window(0, 1)
-    halo(0).wait_recv()
+    halo_here(0)
     window(halo_lr[0].reshape(CHUNK, C), 1)
     attend_window(1, 1)
 
@@ -251,14 +278,14 @@
     for i in range(2):
         ring(i).start()
     across(0).start()
-    halo(1).start()
+    halo_start(1)
     for i in (2, 3):
-        halo(i).wait_recv()
+        halo_here(i)
     for i in range(4, 8):
-        halo(i).start()
+        halo_start(i)
     window(halo_s[:2].reshape(CHUNK, C), 2)
     for i in (4, 5):
-        halo(i).wait_recv()
+        halo_here(i)
     window(halo_s[2:4].reshape(CHUNK, C), 3)
     attend_window(2, 2)
 
@@ -335,23 +362,13 @@
     each(2, 4, sub_chunk)
     attend_sub(0, 5, 2, 2)
 
-    halo(1).wait_recv()
-    window(halo_lr[1].reshape(CHUNK, C), 4)
-    attend_window(4, 1)
+    for i in (1, 2):
+        crossed(i).wait_recv()
+    each(4, 6, sub_chunk)
     for i in (2, 3):
         ringed(i).wait_recv()
     across(3).start()
-    for i in (6, 7):
-        halo(i).wait_recv()
-    window(halo_s[4:].reshape(CHUNK, C), 5)
-    attend_window(5, 1)
-    for j in range(5):
-        both = [acc[2 * j + b, :HD] / acc[2 * j + b, HD : HD + 1] for b in range(2)]
-        local[:, j * 128 : (j + 1) * 128] = jnp.concatenate(both, axis=0).T
-
-    for i in (1, 2):
-        crossed(i).wait_recv()
-    each(4, 7, sub_chunk)
+    sub_chunk(6)
     crossed(3).wait_recv()
     sub_chunk(7)
     for j in range(3):
@@ -365,6 +382,16 @@
         each(1, 32, lambda k: give(j, k).start())
         ret[core, j, me] = dil[j, core * 16 + me]
 
+    halo_here(1)
+    window(halo_lr[1].reshape(CHUNK, C), 4)
+    for i in (6, 7):
+        halo_here(i)
+    window(halo_s[4:].reshape(CHUNK, C), 5)
+    attend_window(4, 2)
+    for j in range(5):
+        both = [acc[2 * j + b, :HD] / acc[2 * j + b, HD : HD + 1] for b in range(2)]
+        local[:, j * 128 : (j + 1) * 128] = jnp.concatenate(both, axis=0).T
+
     def position(ref, natural_of):
         cols = jnp.where(
             natural_of((TOK, 16), 0) % 16 == lax.broadcasted_iota(jnp.int32, (TOK, 16), 1), 1.0, 0.0
@@ -407,7 +434,7 @@
 
     each(1, 16, lambda k: exchange(k).wait_send())
     for i in range(8):
-        halo(i).wait_send()
+        halo_sent(i)
     for i in range(4):
         ring(i).wait_send()
         across(i).wait_send()

time: 109 us -> 108 us (level)
  the two profiles are of different devices: /device:TPU:1 before, /device:TPU:2 now
where the time goes in v3:
time: 108 us
  Pallas kernels  106 us (98%)
  local copies, waits for them, and re-layouts  1.98 us (2%)
    pallas_call x1, Pallas kernels, shards(): pl.pallas_call(kernel, out_shape=jax.ShapeDtypeStruct((TOK, C), BF), in_s...  106 us

profile of v3, /device:TPU:2, one launch (start us, length us, event | category | flops | bytes accessed | tf_op | source)
XLA Modules:
  0.0 108.3 jit_solution(17974272313109641519)
XLA Ops:
  0.0 106.3 %shard_map.91 = bf16[512,640]{1,0:T(8,128)(2,1)} custom-call(bf16[512,640]{1,0:T(8,128)(2,1)} %bitcast.6, bf16[128,640]{1,0:T(8,128)(2,1)} %bitcast.7, f32[16,32]{1,0:T(8,128)} %bitcast.8, f32[16,32]{1,0:T(8,128)} %bitcast.9, f32[640]{0:T(1024)} %gain_ref.1, bf16[640,640]{1,0:T(8,128)(2,1)} %wq_ref.1, bf16[640,640]{1,0:T(8,128)(2,1)} %wk_ref.1, ...), custom_call_target="tpu_custom_call" | custom-call | tf_op jit(solution)/shard_map/pallas_call | solution.py:448
  106.3 2.0 %copy.11 = bf16[1,32,16,640]{3,2,1,0:T(8,128)(2,1)} copy(bf16[1,32,16,640]{3,2,1,0:T(8,128)(2,1)} %bitcast.5) | data formatting | bytes 1310720

commit v4 on v3

--- a/solution.py
+++ b/solution.py
@@ -278,16 +278,6 @@
     for i in range(2):
         ring(i).start()
     across(0).start()
-    halo_start(1)
-    for i in (2, 3):
-        halo_here(i)
-    for i in range(4, 8):
-        halo_start(i)
-    window(halo_s[:2].reshape(CHUNK, C), 2)
-    for i in (4, 5):
-        halo_here(i)
-    window(halo_s[2:4].reshape(CHUNK, C), 3)
-    attend_window(2, 2)
 
     wkd[:, :256] = wk_ref[:, pl.ds(pl.multiple_of(core * 384, 128), 256)]
     wkd[:, 256:] = wk_ref[:, 256:384]
@@ -298,15 +288,6 @@
     qd[...] = jnp.zeros_like(qd)
     max_d[...] = jnp.full_like(max_d, NEG)
     acc_d[...] = jnp.zeros_like(acc_d)
-
-    crossed(0).wait_recv()
-    for c in range(2):
-        tokens = gat[z, c].reshape(CHUNK, C)
-        part = dot_nt(wqd[...], tokens).astype(BF)
-        cols = slice(c * CHUNK, (c + 1) * CHUNK)
-        for i in range(4):
-            qd[i, i % 2 * HD : i % 2 * HD + HD, cols] = part[i * HD : (i + 1) * HD]
-        qd[4, pl.ds(pl.multiple_of(core * HD, HD), HD), cols] = part[256:]
 
     def sub_chunk(g):
         plane = jnp.where(g < 2, 0, jnp.where(g > 5, 2, jnp.where(g % 2 == 0, 3, 1)))
@@ -352,8 +333,33 @@
 
         pipeline(chunks * heads, scores, weigh)
 
-    each(0, 2, sub_chunk)
+    def sub_queries(c):
+        tokens = gat[z, c].reshape(CHUNK, C)
+        part = dot_nt(wqd[...], tokens).astype(BF)
+        cols = pl.ds(pl.multiple_of(c * CHUNK, CHUNK), CHUNK)
+        for i in range(4):
+            qd[i, i % 2 * HD : i % 2 * HD + HD, cols] = part[i * HD : (i + 1) * HD]
+        qd[4, pl.ds(pl.multiple_of(core * HD, HD), HD), cols] = part[256:]
+
+    sub_queries(core)
+    sub_chunk(0)
+    crossed(0).wait_recv()
+    sub_queries(1 - core)
+    sub_chunk(1)
     attend_sub(0, 5, 0, 2)
+
+    for i in (2, 3):
+        halo_here(i)
+    for i in (4, 5):
+        halo_start(i)
+    halo_start(1)
+    for i in (6, 7):
+        halo_start(i)
+    window(halo_s[:2].reshape(CHUNK, C), 2)
+    for i in (4, 5):
+        halo_here(i)
+    window(halo_s[2:4].reshape(CHUNK, C), 3)
+    attend_window(2, 2)
 
     for i in (0, 1):
         ringed(i).wait_recv()

time: 108 us -> 96.2 us (0.89)
  the two profiles are of different devices: /device:TPU:2 before, /device:TPU:1 now
where the time goes in v4:
time: 96.2 us; the launch traced here: 96 us
  Pallas kernels  94 us (98%)
  local copies, waits for them, and re-layouts  1.98 us (2%)
    pallas_call x1, Pallas kernels, shards(): pl.pallas_call(kernel, out_shape=jax.ShapeDtypeStruct((TOK, C), BF), in_s...  94 us
    unnamed x1, local copies, waits for them, and re-layouts  1.98 us

profile of v4, /device:TPU:1, one launch (start us, length us, event | category | flops | bytes accessed | tf_op | source)
XLA Modules:
  0.0 96.0 jit_solution(13652090651906704229)
XLA Ops:
  0.0 94.0 %shard_map.91 = bf16[512,640]{1,0:T(8,128)(2,1)} custom-call(bf16[512,640]{1,0:T(8,128)(2,1)} %bitcast.6, bf16[128,640]{1,0:T(8,128)(2,1)} %bitcast.7, f32[16,32]{1,0:T(8,128)} %bitcast.8, f32[16,32]{1,0:T(8,128)} %bitcast.9, f32[640]{0:T(1024)} %gain_ref.1, bf16[640,640]{1,0:T(8,128)(2,1)} %wq_ref.1, bf16[640,640]{1,0:T(8,128)(2,1)} %wk_ref.1, ...), custom_call_target="tpu_custom_call" | custom-call | tf_op jit(solution)/shard_map/pallas_call | solution.py:454
  94.1 2.0 %copy.11 = bf16[1,32,16,640]{3,2,1,0:T(8,128)(2,1)} copy(bf16[1,32,16,640]{3,2,1,0:T(8,128)(2,1)} %bitcast.5) | data formatting | bytes 1310720
